TPU v7x, 512 devices: a whole 4x4x16 slice. The times are simulated.
512 devices in a mesh: tm: 8 (over x, y_hi), tile: 64 (over z, y_lo, core).
Axes of the slice: x: 4, y: 4 (y_hi: 2, y_lo: 2; y = y_hi * 2 + y_lo), z: 16, core: 2. Of those that a mesh axis runs over, the one named last changes fastest.
Arguments:
- blocks: float32 [8, 320, 128, 128], P('tm', None, 'tile'), may hold values from -16 to 16
- coef_first: float32 [128, 128], P('tile'), may hold values from 0.5 to 2
- coef_second: float32 [128, 128], P('tile'), may hold values from 0.5 to 2
- wet: int32 [128, 128], P('tile'), may hold values 0 or 1
Outputs:
- hessian: float32 [8, 320, 320], P('tm', 'tile')
All inputs are finite; a program needn't handle non-finite values. No bound on the sum of `wet` on one device may be relied on, other than what follows from the above.
Results may differ from a plain program's by a relative error of at most 0.000088.
Values sent between devices are 32-bit elements; how exact they have to be, the bound alone decides.
No kernel may reach another device: no remote copies, remote signals or barrier semaphores. Data moves between devices by JAX's collectives and lax.ppermute only.
A program may use at most 64 MiB of HBM per device.

v0:
```python
import jax
import jax.numpy as jnp
from jax import lax
from jax.sharding import Mesh
from jax.sharding import PartitionSpec as P

TILE = ("tile_0", "tile_1", "tile_2")


def extended(block, sides, width):
    for axis, dim in sides:
        count = lax.axis_size(axis)
        forward = [(i, i + 1) for i in range(count - 1)]
        backward = [(target, source) for source, target in forward]
        low = lax.ppermute(
            lax.slice_in_dim(block, block.shape[dim] - width, None, axis=dim), axis, forward
        )
        high = lax.ppermute(lax.slice_in_dim(block, 0, width, axis=dim), axis, backward)
        block = jnp.concatenate([low, block, high], axis=dim)
    return block


def reduced_to_own(blocks, axes, sequence):
    lengths = [lax.axis_size(a) for a in axes]
    blocks = blocks.reshape(*lengths, *blocks.shape[1:])
    blocks = blocks.transpose(*sequence, *range(len(axes), blocks.ndim))
    blocks = blocks.reshape(-1, *blocks.shape[len(axes) :])
    for k in sequence:
        blocks = lax.psum_scatter(blocks, axes[k], scatter_dimension=0, tiled=True)
    return blocks[0]


def split_up(array, dim, length):
    lengths = array.shape
    blocks = array.reshape(*lengths[:dim], length, lengths[dim] // length, *lengths[dim + 1 :])
    return jnp.moveaxis(blocks, dim, 0)


def summed_rows(array, axes, sequence, dim):
    length = lax.axis_size(axes)
    return reduced_to_own(split_up(array, dim, length), axes, sequence)


def sent_and_summed(array, axis, dim):
    length = lax.axis_size(axis)
    blocks = lax.all_to_all(split_up(array, dim, length), axis, 0, 0, tiled=True)
    return jnp.sum(blocks, axis=0)


def apply_sweep(wide, coef):
    inner = wide[..., 1:-1, :]
    widths = ((0, 0),) * (inner.ndim - 1) + ((1, 1),)
    padded = jnp.pad(inner, widths)
    beside = wide[..., 2:, :] + wide[..., :-2, :] + padded[..., 2:] + padded[..., :-2]
    return coef * inner + 0.2 * beside


def shards(blocks, coef_first, coef_second, wet):
    block = blocks[0]
    wetf = wet.astype(jnp.float32)
    fields = jnp.stack([coef_first, wetf])
    fields_wide = extended(fields, ((TILE, 1),), 2)
    deep = extended(block * wetf, ((TILE, 1),), 2)
    first = apply_sweep(deep, fields_wide[0][1:-1])
    second = apply_sweep(first * fields_wide[1][1:-1], coef_second)
    obs_rows = second.shape[0]
    own = second.reshape(obs_rows, second.shape[1] * second.shape[2])
    groups = lax.axis_size("tm")
    pieces = [None] * groups
    regrouped = lax.all_to_all(own[None], "tm", split_axis=2, concat_axis=0, tiled=True)
    for offset in range(groups):
        partner = jnp.roll(regrouped, -offset, axis=0)
        pieces[offset] = jnp.einsum(
            "gop,gqp->oq",
            regrouped,
            partner,
            precision=lax.Precision.HIGHEST,
            preferred_element_type=jnp.float32,
        )
    stacked = jnp.stack(pieces)
    count = jnp.float32(own.shape[1] * lax.axis_size(TILE))
    shared = summed_rows(stacked, TILE, (2, 0, 1), 1)
    mine = sent_and_summed(shared, "tm", 0)
    return mine / count


def solution(mesh):
    finer = Mesh(
        mesh.devices.reshape(mesh.shape["tm"], 16, 2, 2), ("tm", "tile_0", "tile_1", "tile_2")
    )
    in_specs = (P("tm", None, TILE, None), P(TILE, None), P(TILE, None), P(TILE, None))
    out_specs = P("tm", TILE, None)
    return jax.shard_map(
        shards, mesh=finer, in_specs=in_specs, out_specs=out_specs, check_vma=False
    )
```

profile of v0, /device:TPU:32, one launch (start us, length us, event | category | flops | bytes accessed | tf_op | source)
XLA Modules:
  0.0 220.7 jit_solution(11319167961660188351)
XLA Ops:
  6.5 0.0 reduce-scatter.7.cloned.1.call-start
  6.5 0.7 convert_bitcast_fusion
  7.2 1.1 bitcast_multiply_fusion
  8.3 1.9 collective-permute-start.2
  10.2 4.5 %collective-permute-start.3 = (f32[320,2,128]{2,1,0:T(2,128)S(1)}, f32[320,2,128]{2,1,0:T(2,128)S(1)}, u32[]{:S(2)}, u32[]{:S(2)}) collective-permute-start(f32[320,2,128]{2,1,0:T(2,128)S(1)} %bitcast_multiply_fusion), channel_id=1, source_target_pairs={{1,0},{2,1},{3,2},{4,3},{5,4},{6,5},{7,6},{8,7},{9,8},{10,9},{11,1... | collective-permute-start | bytes 983048 | tf_op jit(solution)/shard_map/ppermute | solution.py:18
  14.8 0.7 pad_maximum_fusion.5
  15.5 1.9 collective-permute-start
  17.4 4.5 %collective-permute-start.1 = (f32[2,2,128]{2,1,0:T(2,128)S(1)}, f32[2,2,128]{2,1,0:T(2,128)S(1)}, u32[]{:S(2)}, u32[]{:S(2)}) collective-permute-start(f32[2,2,128]{2,1,0:T(2,128)S(1)} %pad_maximum_fusion.5), channel_id=1, source_target_pairs={{1,0},{2,1},{3,2},{4,3},{5,4},{6,5},{7,6},{8,7},{9,8},{10,9},{11,1... | collective-permute-start | bytes 6152 | tf_op jit(solution)/shard_map/ppermute | solution.py:18
  21.9 0.0 collective-permute-done
  22.0 1.3 collective-permute-done.1
  23.2 0.7 maximum_bitcast_fusion.14
  23.9 0.0 collective-permute-done.2
  23.9 0.0 collective-permute-done.3
  24.0 0.5 pad_maximum_fusion
  24.5 0.9 fusion.12
  25.3 0.2 slice.176
  25.5 0.0 copy-done.7
  25.5 0.7 multiply_add_fusion
  26.3 0.3 broadcast_in_dim_reshape.3
  26.5 0.4 copy.53
  27.0 16.5 %all_to_all.23 = f32[1,320,256]{1,0,2:T(1,128)S(1)} all-to-all(f32[1,320,256]{1,0,2:T(1,128)S(1)} %copy.53), channel_id=1, replica_groups=mesh['tm'=8,'tile_0'=16,'tile_1'=2,'tile_2'=2] {'tm'}, dimensions={2} | all-to-all | bytes 655360 | tf_op jit(solution)/shard_map/all_to_all | solution.py:70
  43.4 0.1 slice_bitcast_fusion
  43.5 0.6 slice_bitcast_fusion.13
  44.1 0.8 slice_bitcast_fusion.2
  44.9 0.7 slice_bitcast_fusion.10
  45.6 0.8 slice_bitcast_fusion.4
  46.4 0.8 slice_bitcast_fusion.8
  47.2 0.7 slice_bitcast_fusion.7
  47.9 0.5 copy.54
  48.4 0.4 copy.55
  48.8 0.0 copy-start.2
  48.8 0.0 copy-start.5
  48.8 0.0 copy-start.3
  48.8 0.0 copy-start.1
  48.8 0.0 copy-start.4
  48.8 1.4 fusion.7
  50.3 2.3 %fusion.6 = f32[8,64,5,320]{3,1,2,0:T(8,128)S(1)} fusion(f32[8,64,5,320]{3,1,2,0:T(8,128)S(1)} %fusion.7, f32[64,5,8,32]{0,3,2,1:T(8,128)S(1)} %copy.55, f32[1,320,32]{1,2,0:T(8,128)} %slice_bitcast_fusion.13, f32[7,320,32]{1,2,0:T(8,128)S(1)} %get-tuple-element.6), kind=kOutput, calls=%fused_computation.15 | convolution fusion | flops 314654720 | bytes 1531904 | tf_op jit(solution)/shard_map/gop,gqp->oq/dot_general | solution.py:73
  52.5 2.5 %fusion.5 = f32[8,64,5,320]{3,1,2,0:T(8,128)S(1)} fusion(f32[8,64,5,320]{3,1,2,0:T(8,128)S(1)} %fusion.6, f32[64,5,8,32]{0,3,2,1:T(8,128)S(1)} %copy.55, f32[2,320,32]{1,2,0:T(8,128)} %get-tuple-element.8, f32[6,320,32]{1,2,0:T(8,128)} %get-tuple-element.10), kind=kOutput, calls=%fused_computation.13 | convolution fusion | flops 314654720 | bytes 1474560 | tf_op jit(solution)/shard_map/gop,gqp->oq/dot_general | solution.py:73
  55.0 0.0 copy-done.2
  55.0 0.0 copy-done.5
  55.0 1.4 fusion.4
  56.4 0.0 copy-done.3
  56.4 1.4 fusion.3
  57.9 0.0 copy-done.1
  57.9 0.0 copy-done.4
  57.9 1.4 fusion.2
  59.3 0.0 copy-done.6
  59.3 1.4 fusion.1
  60.8 1.4 fusion
  62.2 1.9 copy-done
  64.1 5.6 %reshape.89 = f32[16,2,2,8,5,320]{5,2,1,0,4,3:T(2,128)} reshape(f32[64,8,5,320]{3,0,2,1:T(8,128)} %bitcast.152) | data formatting | bytes 6553600 | tf_op jit(solution)/shard_map/reshape | solution.py:25
  69.7 6.2 %copy.64 = f32[16,2,2,8,5,320]{5,3,4,1,0,2:T(8,128)} copy(f32[16,2,2,8,5,320]{5,2,1,0,4,3:T(2,128)} %reshape.89) | data formatting | bytes 6553600 | tf_op jit(solution)/shard_map/reshape | solution.py:25
  75.9 0.0 reduce-scatter.7.cloned.1.call-update
  75.9 0.0 reduce-scatter.9.cloned.1.call-start
  76.0 24.5 %reduce-scatter.7.cloned.1.call-done = f32[32,8,5,320]{3,1,2,0:T(8,128)} async-done(((f32[64,8,5,320]{3,1,2,0:T(8,128)}), f32[32,8,5,320]{3,1,2,0:T(8,128)}) %reduce-scatter.7.cloned.1.call-update) | async-done | bytes 1638416 | tf_op jit(solution)/shard_map/reduce_scatter | solution.py:29
  100.5 0.0 reduce-scatter.9.cloned.1.call-update
  100.5 0.0 reduce-scatter.11.cloned.1.call-start
  100.6 76.6 %reduce-scatter.9.cloned.1.call-done = f32[2,8,5,320]{3,1,2,0:T(8,128)} async-done(((f32[32,8,5,320]{3,1,2,0:T(8,128)}), f32[2,8,5,320]{3,1,2,0:T(8,128)}) %reduce-scatter.9.cloned.1.call-update) | async-done | bytes 102416 | tf_op jit(solution)/shard_map/reduce_scatter | solution.py:29
  177.1 0.0 reduce-scatter.11.cloned.1.call-update
  177.2 21.5 %reduce-scatter.11.cloned.1.call-done = f32[1,8,5,320]{3,1,2,0:T(8,128)} async-done(((f32[2,8,5,320]{3,1,2,0:T(8,128)}), f32[1,8,5,320]{3,1,2,0:T(8,128)}) %reduce-scatter.11.cloned.1.call-update) | async-done | bytes 51216
  198.7 0.9 copy.65
  199.5 14.0 %all_to_all.24 = f32[8,1,5,320]{3,1,2,0:T(1,128)S(1)} all-to-all(f32[8,1,5,320]{3,1,2,0:T(1,128)S(1)} %copy.65), channel_id=1, replica_groups=mesh['tm'=8,'tile_0'=16,'tile_1'=2,'tile_2'=2] {'tm'}, dimensions={0} | all-to-all | bytes 102400 | tf_op jit(solution)/shard_map/all_to_all | solution.py:46
  213.5 0.1 reduce_sum.9
  213.6 0.6 div.10
  (6 shorter events, 0.0 us)
Async XLA Ops:
  6.5 19.0 %copy-start.7 = (f32[2,128]{1,0:T(2,128)S(1)}, f32[2,128]{1,0:T(2,128)}, u32[]{:S(2)}) copy-start(f32[2,128]{1,0:T(2,128)} %param.6) | copy-start | bytes 3076
  6.5 93.9 %reduce-scatter.7.cloned.1.call-start = ((), (), s32[]{:S(2)}) async-start(), calls=%async_computation.5 | async-start | bytes 5898240 | tf_op jit(solution)/shard_map/reduce_scatter | solution.py:29
  8.3 15.6 %collective-permute-start.2 = (f32[320,2,128]{2,1,0:T(2,128)S(1)}, f32[320,2,128]{2,1,0:T(2,128)S(1)}, u32[]{:S(2)}, u32[]{:S(2)}) collective-permute-start(f32[320,2,128]{2,1,0:T(2,128)S(1)} %bitcast_multiply_fusion), channel_id=1, source_target_pairs={{0,1},{1,2},{2,3},{3,4},{4,5},{5,6},{6,7},{7,8},{8,9},{9,10},{10,1... | collective-permute-start | bytes 983048 | tf_op jit(solution)/shard_map/ppermute | solution.py:15
  10.2 13.7 %collective-permute-start.3 = (f32[320,2,128]{2,1,0:T(2,128)S(1)}, f32[320,2,128]{2,1,0:T(2,128)S(1)}, u32[]{:S(2)}, u32[]{:S(2)}) collective-permute-start(f32[320,2,128]{2,1,0:T(2,128)S(1)} %bitcast_multiply_fusion), channel_id=1, source_target_pairs={{1,0},{2,1},{3,2},{4,3},{5,4},{6,5},{7,6},{8,7},{9,8},{10,9},{11,1... | collective-permute-start | bytes 983048 | tf_op jit(solution)/shard_map/ppermute | solution.py:18
  15.5 6.5 %collective-permute-start = (f32[2,2,128]{2,1,0:T(2,128)S(1)}, f32[2,2,128]{2,1,0:T(2,128)S(1)}, u32[]{:S(2)}, u32[]{:S(2)}) collective-permute-start(f32[2,2,128]{2,1,0:T(2,128)S(1)} %pad_maximum_fusion.5), channel_id=1, source_target_pairs={{0,1},{1,2},{2,3},{3,4},{4,5},{5,6},{6,7},{7,8},{8,9},{9,10},{10,1... | collective-permute-start | bytes 6152 | tf_op jit(solution)/shard_map/ppermute | solution.py:15
  17.4 5.8 %collective-permute-start.1 = (f32[2,2,128]{2,1,0:T(2,128)S(1)}, f32[2,2,128]{2,1,0:T(2,128)S(1)}, u32[]{:S(2)}, u32[]{:S(2)}) collective-permute-start(f32[2,2,128]{2,1,0:T(2,128)S(1)} %pad_maximum_fusion.5), channel_id=1, source_target_pairs={{1,0},{2,1},{3,2},{4,3},{5,4},{6,5},{7,6},{8,7},{9,8},{10,9},{11,1... | collective-permute-start | bytes 6152 | tf_op jit(solution)/shard_map/ppermute | solution.py:18
  48.8 6.2 %copy-start.2 = (f32[5,320,32]{1,2,0:T(8,128)S(1)}, f32[5,320,32]{1,2,0:T(8,128)}, u32[]{:S(2)}) copy-start(f32[5,320,32]{1,2,0:T(8,128)} %get-tuple-element.14) | copy-start | bytes 614404
  48.8 6.2 %copy-start.5 = (f32[3,320,32]{1,2,0:T(8,128)S(1)}, f32[3,320,32]{1,2,0:T(8,128)}, u32[]{:S(2)}) copy-start(f32[3,320,32]{1,2,0:T(8,128)} %get-tuple-element.12) | copy-start | bytes 368644
  48.8 7.6 %copy-start.3 = (f32[4,320,32]{1,2,0:T(8,128)S(1)}, f32[4,320,32]{1,2,0:T(8,128)}, u32[]{:S(2)}) copy-start(f32[4,320,32]{1,2,0:T(8,128)} %get-tuple-element.16) | copy-start | bytes 491524
  48.8 9.1 %copy-start.1 = (f32[5,320,32]{1,2,0:T(8,128)S(1)}, f32[5,320,32]{1,2,0:T(8,128)}, u32[]{:S(2)}) copy-start(f32[5,320,32]{1,2,0:T(8,128)} %get-tuple-element.13) | copy-start | bytes 614404
  48.8 9.1 %copy-start.4 = (f32[3,320,32]{1,2,0:T(8,128)S(1)}, f32[3,320,32]{1,2,0:T(8,128)}, u32[]{:S(2)}) copy-start(f32[3,320,32]{1,2,0:T(8,128)} %get-tuple-element.11) | copy-start | bytes 368644
  50.3 9.1 %copy-start.6 = (f32[2,320,32]{1,2,0:T(8,128)S(1)}, f32[2,320,32]{1,2,0:T(8,128)}, u32[]{:S(2)}) copy-start(f32[2,320,32]{1,2,0:T(8,128)} %get-tuple-element.7) | copy-start | bytes 245764
  62.2 1.9 copy-start
  75.9 101.2 %reduce-scatter.9.cloned.1.call-start = ((), (), s32[]{:S(2)}) async-start(), calls=%async_computation.6 | async-start | bytes 2088960 | tf_op jit(solution)/shard_map/reduce_scatter | solution.py:29
  100.5 98.1 %reduce-scatter.11.cloned.1.call-start = ((), (), s32[]{:S(2)}) async-start(), calls=%async_computation.7 | async-start | bytes 184320
Sparse Core Ops, SparseCore 0:
  76.0 24.3 reduce-scatter.6
  103.6 73.5 reduce-scatter.8
  179.9 18.7 reduce-scatter.10
where the time goes:
time: 221 us
  waiting for transfers between devices  124 us (56%)
  blocking collectives  30.4 us (14%)
  local copies, waits for them, and re-layouts  21.4 us (10%)
  between operations  13.4 us (6%)
  matrix products  13.3 us (6%)
  starting transfers between devices  13 us (6%)
  other arithmetic  5.33 us (2%)
    reduce_scatter x2, waiting for transfers between devices, reduced_to_own(): blocks = lax.psum_scatter(blocks, axes[k], scatter_dimension=0, tiled=True)  101 us
    unnamed x4, waiting for transfers between devices  21.5 us
    all_to_all x1, blocking collectives, shards(): lax.all_to_all(own[None], 'tm', split_axis=2, concat_axis=0, tiled=True)  16.5 us
    all_to_all x1, blocking collectives, sent_and_summed(): lax.all_to_all(split_up(array, dim, length), axis, 0, 0, tiled=True)  14 us
    dot_general x8, matrix products, shards(): jnp.einsum('gop,gqp->oq', regrouped, partner, precision=lax.Precision.HIG...  13.3 us
    reshape x2, local copies, waits for them, and re-layouts, reduced_to_own(): blocks = blocks.reshape(*lengths, *blocks.shape[1:])  11.8 us
    ppermute x2, starting transfers between devices, extended(): lax.ppermute(lax.slice_in_dim(block, 0, width, axis=dim), axis, backward)  9.08 us
    slice x8, local copies, waits for them, and re-layouts, shards(): partner = jnp.roll(regrouped, -offset, axis=0)  4.42 us
  transfers between devices with their start and end apart: 7, of which 4 were waited for; matrix products, arithmetic and copies ran while one was open for 1% of the time, Pallas kernels for 0%

commit v1 on v0

--- a/solution.py
+++ b/solution.py
@@ -67,7 +67,10 @@
     own = second.reshape(obs_rows, second.shape[1] * second.shape[2])
     groups = lax.axis_size("tm")
     pieces = [None] * groups
-    regrouped = lax.all_to_all(own[None], "tm", split_axis=2, concat_axis=0, tiled=True)
+    regrouped = jnp.concatenate(
+        lax.all_to_all(jnp.stack(jnp.split(own[None], lax.axis_size("tm"), axis=2)), "tm", 0, 0),
+        axis=0,
+    )
     for offset in range(groups):
         partner = jnp.roll(regrouped, -offset, axis=0)
         pieces[offset] = jnp.einsum(

time: 221 us -> 219 us (level)
    slice x8 -> x7, local copies, waits for them, and re-layouts: 4.42 us -> 3.83 us  [shards(): partner = jnp.roll(regrouped, -offset, axis=0)]
where the time goes in v1:
time: 219 us
  waiting for transfers between devices  124 us (57%)
  blocking collectives  30.4 us (14%)
  local copies, waits for them, and re-layouts  20.4 us (9%)
  between operations  13.4 us (6%)
  starting transfers between devices  13 us (6%)
  matrix products  12.5 us (6%)
  other arithmetic  5.35 us (2%)
    reduce_scatter x2, waiting for transfers between devices, reduced_to_own(): blocks = lax.psum_scatter(blocks, axes[k], scatter_dimension=0, tiled=True)  101 us
    unnamed x4, waiting for transfers between devices  21.5 us
    all_to_all x1, blocking collectives, shards(): lax.all_to_all(jnp.stack(jnp.split(own[None], lax.axis_size('tm'), axis=2...  16.5 us
    all_to_all x1, blocking collectives, sent_and_summed(): lax.all_to_all(split_up(array, dim, length), axis, 0, 0, tiled=True)  14 us
    dot_general x8, matrix products, shards(): jnp.einsum('gop,gqp->oq', regrouped, partner, precision=lax.Precision.HIG...  12.5 us
    reshape x2, local copies, waits for them, and re-layouts, reduced_to_own(): blocks = blocks.reshape(*lengths, *blocks.shape[1:])  11.8 us
    ppermute x2, starting transfers between devices, extended(): lax.ppermute(lax.slice_in_dim(block, 0, width, axis=dim), axis, backward)  9.08 us
  transfers between devices with their start and end apart: 7, of which 4 were waited for; matrix products, arithmetic and copies ran while one was open for 1% of the time, Pallas kernels for 0%

profile of v1, /device:TPU:32, one launch (start us, length us, event | category | flops | bytes accessed | tf_op | source)
XLA Modules:
  0.0 218.8 jit_solution(17421382869644584652)
XLA Ops:
  6.5 0.0 copy-start.7
  6.5 0.0 reduce-scatter.7.cloned.1.call-start
  6.5 0.7 convert_bitcast_fusion
  7.2 1.1 bitcast_multiply_fusion
  8.3 1.9 collective-permute-start.2
  10.2 4.5 %collective-permute-start.3 = (f32[320,2,128]{2,1,0:T(2,128)S(1)}, f32[320,2,128]{2,1,0:T(2,128)S(1)}, u32[]{:S(2)}, u32[]{:S(2)}) collective-permute-start(f32[320,2,128]{2,1,0:T(2,128)S(1)} %bitcast_multiply_fusion), channel_id=1, source_target_pairs={{1,0},{2,1},{3,2},{4,3},{5,4},{6,5},{7,6},{8,7},{9,8},{10,9},{11,1... | collective-permute-start | bytes 983048 | tf_op jit(solution)/shard_map/ppermute | solution.py:18
  14.8 0.7 pad_maximum_fusion.5
  15.5 1.9 collective-permute-start
  17.4 4.5 %collective-permute-start.1 = (f32[2,2,128]{2,1,0:T(2,128)S(1)}, f32[2,2,128]{2,1,0:T(2,128)S(1)}, u32[]{:S(2)}, u32[]{:S(2)}) collective-permute-start(f32[2,2,128]{2,1,0:T(2,128)S(1)} %pad_maximum_fusion.5), channel_id=1, source_target_pairs={{1,0},{2,1},{3,2},{4,3},{5,4},{6,5},{7,6},{8,7},{9,8},{10,9},{11,1... | collective-permute-start | bytes 6152 | tf_op jit(solution)/shard_map/ppermute | solution.py:18
  21.9 0.0 collective-permute-done
  22.0 1.3 collective-permute-done.1
  23.2 0.7 maximum_bitcast_fusion.14
  23.9 0.0 collective-permute-done.2
  23.9 0.0 collective-permute-done.3
  24.0 0.5 pad_maximum_fusion
  24.5 0.9 fusion.12
  25.3 0.2 slice.176
  25.5 0.0 copy-done.7
  25.5 0.8 multiply_add_fusion
  26.3 0.2 copy.65
  26.6 16.5 %all_to_all.10 = f32[8,1,320,32]{2,3,1,0:T(8,128)S(1)} all-to-all(f32[8,1,320,32]{2,3,1,0:T(8,128)S(1)} %fusion.30), channel_id=1, replica_groups=mesh['tm'=8,'tile_0'=16,'tile_1'=2,'tile_2'=2] {'tm'}, dimensions={0} | all-to-all | bytes 655360 | tf_op jit(solution)/shard_map/all_to_all | solution.py:71
  43.0 0.1 slice_bitcast_fusion
  43.1 0.8 slice_bitcast_fusion.2
  43.9 0.7 slice_bitcast_fusion.10
  44.6 0.8 slice_bitcast_fusion.4
  45.4 0.8 slice_bitcast_fusion.8
  46.2 0.7 slice_bitcast_fusion.7
  46.9 0.5 copy.66
  47.4 0.4 copy.67
  47.8 0.0 copy-start.2
  47.8 0.0 copy-start.5
  47.8 0.0 copy-start.3
  47.8 0.0 copy-start.1
  47.8 0.0 copy-start.4
  47.9 1.4 fusion.7
  49.3 0.0 copy-start.6
  49.3 1.4 fusion.6
  50.7 2.5 %fusion.5 = f32[8,64,5,320]{3,1,2,0:T(8,128)S(1)} fusion(f32[8,64,5,320]{3,1,2,0:T(8,128)S(1)} %fusion.6, f32[64,5,8,32]{0,3,2,1:T(8,128)S(1)} %copy.67, f32[2,320,32]{1,2,0:T(8,128)} %get-tuple-element.10, f32[6,320,32]{1,2,0:T(8,128)} %get-tuple-element.12), kind=kOutput, calls=%fused_computation.13 | convolution fusion | flops 314654720 | bytes 1474560 | tf_op jit(solution)/shard_map/gop,gqp->oq/dot_general | solution.py:76
  53.2 0.0 copy-done.2
  53.2 0.0 copy-done.5
  53.2 1.4 fusion.4
  54.6 0.0 copy-done.3
  54.6 1.4 fusion.3
  56.1 0.0 copy-done.1
  56.1 0.0 copy-done.4
  56.1 1.4 fusion.2
  57.5 0.0 copy-done.6
  57.5 1.4 fusion.1
  58.9 1.4 fusion
  60.4 1.9 copy-done
  62.3 5.6 %reshape.93 = f32[16,2,2,8,5,320]{5,2,1,0,4,3:T(2,128)} reshape(f32[64,8,5,320]{3,0,2,1:T(8,128)} %bitcast.185) | data formatting | bytes 6553600 | tf_op jit(solution)/shard_map/reshape | solution.py:25
  67.8 6.3 %copy.87 = f32[16,2,2,8,5,320]{5,3,4,1,0,2:T(8,128)} copy(f32[16,2,2,8,5,320]{5,2,1,0,4,3:T(2,128)} %reshape.93) | data formatting | bytes 6553600 | tf_op jit(solution)/shard_map/reshape | solution.py:25
  74.1 0.0 reduce-scatter.7.cloned.1.call-update
  74.1 0.0 reduce-scatter.9.cloned.1.call-start
  74.2 24.5 %reduce-scatter.7.cloned.1.call-done = f32[32,8,5,320]{3,1,2,0:T(8,128)} async-done(((f32[64,8,5,320]{3,1,2,0:T(8,128)}), f32[32,8,5,320]{3,1,2,0:T(8,128)}) %reduce-scatter.7.cloned.1.call-update) | async-done | bytes 1638416 | tf_op jit(solution)/shard_map/reduce_scatter | solution.py:29
  98.7 0.0 reduce-scatter.9.cloned.1.call-update
  98.7 0.0 reduce-scatter.11.cloned.1.call-start
  98.8 76.6 %reduce-scatter.9.cloned.1.call-done = f32[2,8,5,320]{3,1,2,0:T(8,128)} async-done(((f32[32,8,5,320]{3,1,2,0:T(8,128)}), f32[2,8,5,320]{3,1,2,0:T(8,128)}) %reduce-scatter.9.cloned.1.call-update) | async-done | bytes 102416 | tf_op jit(solution)/shard_map/reduce_scatter | solution.py:29
  175.4 0.0 reduce-scatter.11.cloned.1.call-update
  175.4 21.4 %reduce-scatter.11.cloned.1.call-done = f32[1,8,5,320]{3,1,2,0:T(8,128)} async-done(((f32[2,8,5,320]{3,1,2,0:T(8,128)}), f32[1,8,5,320]{3,1,2,0:T(8,128)}) %reduce-scatter.11.cloned.1.call-update) | async-done | bytes 51216
  196.8 0.9 copy.88
  197.7 14.0 %all_to_all.11 = f32[8,1,5,320]{3,1,2,0:T(1,128)S(1)} all-to-all(f32[8,1,5,320]{3,1,2,0:T(1,128)S(1)} %copy.88), channel_id=1, replica_groups=mesh['tm'=8,'tile_0'=16,'tile_1'=2,'tile_2'=2] {'tm'}, dimensions={0} | all-to-all | bytes 102400 | tf_op jit(solution)/shard_map/all_to_all | solution.py:46
  211.6 0.1 reduce_sum.9
  211.7 0.6 div.10
  (11 shorter events, 0.1 us)
Async XLA Ops:
  6.5 19.0 %copy-start.7 = (f32[2,128]{1,0:T(2,128)S(1)}, f32[2,128]{1,0:T(2,128)}, u32[]{:S(2)}) copy-start(f32[2,128]{1,0:T(2,128)} %param.6) | copy-start | bytes 3076
  6.5 92.1 %reduce-scatter.7.cloned.1.call-start = ((), (), s32[]{:S(2)}) async-start(), calls=%async_computation.5 | async-start | bytes 5898240 | tf_op jit(solution)/shard_map/reduce_scatter | solution.py:29
  8.3 15.6 %collective-permute-start.2 = (f32[320,2,128]{2,1,0:T(2,128)S(1)}, f32[320,2,128]{2,1,0:T(2,128)S(1)}, u32[]{:S(2)}, u32[]{:S(2)}) collective-permute-start(f32[320,2,128]{2,1,0:T(2,128)S(1)} %bitcast_multiply_fusion), channel_id=1, source_target_pairs={{0,1},{1,2},{2,3},{3,4},{4,5},{5,6},{6,7},{7,8},{8,9},{9,10},{10,1... | collective-permute-start | bytes 983048 | tf_op jit(solution)/shard_map/ppermute | solution.py:15
  10.2 13.7 %collective-permute-start.3 = (f32[320,2,128]{2,1,0:T(2,128)S(1)}, f32[320,2,128]{2,1,0:T(2,128)S(1)}, u32[]{:S(2)}, u32[]{:S(2)}) collective-permute-start(f32[320,2,128]{2,1,0:T(2,128)S(1)} %bitcast_multiply_fusion), channel_id=1, source_target_pairs={{1,0},{2,1},{3,2},{4,3},{5,4},{6,5},{7,6},{8,7},{9,8},{10,9},{11,1... | collective-permute-start | bytes 983048 | tf_op jit(solution)/shard_map/ppermute | solution.py:18
  15.5 6.5 %collective-permute-start = (f32[2,2,128]{2,1,0:T(2,128)S(1)}, f32[2,2,128]{2,1,0:T(2,128)S(1)}, u32[]{:S(2)}, u32[]{:S(2)}) collective-permute-start(f32[2,2,128]{2,1,0:T(2,128)S(1)} %pad_maximum_fusion.5), channel_id=1, source_target_pairs={{0,1},{1,2},{2,3},{3,4},{4,5},{5,6},{6,7},{7,8},{8,9},{9,10},{10,1... | collective-permute-start | bytes 6152 | tf_op jit(solution)/shard_map/ppermute | solution.py:15
  17.4 5.8 %collective-permute-start.1 = (f32[2,2,128]{2,1,0:T(2,128)S(1)}, f32[2,2,128]{2,1,0:T(2,128)S(1)}, u32[]{:S(2)}, u32[]{:S(2)}) collective-permute-start(f32[2,2,128]{2,1,0:T(2,128)S(1)} %pad_maximum_fusion.5), channel_id=1, source_target_pairs={{1,0},{2,1},{3,2},{4,3},{5,4},{6,5},{7,6},{8,7},{9,8},{10,9},{11,1... | collective-permute-start | bytes 6152 | tf_op jit(solution)/shard_map/ppermute | solution.py:18
  47.8 5.4 %copy-start.2 = (f32[5,320,32]{1,2,0:T(8,128)S(1)}, f32[5,320,32]{1,2,0:T(8,128)}, u32[]{:S(2)}) copy-start(f32[5,320,32]{1,2,0:T(8,128)} %get-tuple-element.16) | copy-start | bytes 614404
  47.8 5.4 %copy-start.5 = (f32[3,320,32]{1,2,0:T(8,128)S(1)}, f32[3,320,32]{1,2,0:T(8,128)}, u32[]{:S(2)}) copy-start(f32[3,320,32]{1,2,0:T(8,128)} %get-tuple-element.14) | copy-start | bytes 368644
  47.8 6.8 %copy-start.3 = (f32[4,320,32]{1,2,0:T(8,128)S(1)}, f32[4,320,32]{1,2,0:T(8,128)}, u32[]{:S(2)}) copy-start(f32[4,320,32]{1,2,0:T(8,128)} %get-tuple-element.18) | copy-start | bytes 491524
  47.8 8.2 %copy-start.1 = (f32[5,320,32]{1,2,0:T(8,128)S(1)}, f32[5,320,32]{1,2,0:T(8,128)}, u32[]{:S(2)}) copy-start(f32[5,320,32]{1,2,0:T(8,128)} %get-tuple-element.15) | copy-start | bytes 614404
  47.8 8.2 %copy-start.4 = (f32[3,320,32]{1,2,0:T(8,128)S(1)}, f32[3,320,32]{1,2,0:T(8,128)}, u32[]{:S(2)}) copy-start(f32[3,320,32]{1,2,0:T(8,128)} %get-tuple-element.13) | copy-start | bytes 368644
  49.3 8.2 %copy-start.6 = (f32[2,320,32]{1,2,0:T(8,128)S(1)}, f32[2,320,32]{1,2,0:T(8,128)}, u32[]{:S(2)}) copy-start(f32[2,320,32]{1,2,0:T(8,128)} %get-tuple-element.9) | copy-start | bytes 245764
  60.4 1.9 copy-start
  74.1 101.2 %reduce-scatter.9.cloned.1.call-start = ((), (), s32[]{:S(2)}) async-start(), calls=%async_computation.6 | async-start | bytes 2088960 | tf_op jit(solution)/shard_map/reduce_scatter | solution.py:29
  98.7 98.1 %reduce-scatter.11.cloned.1.call-start = ((), (), s32[]{:S(2)}) async-start(), calls=%async_computation.7 | async-start | bytes 184320
Sparse Core Ops, SparseCore 0:
  74.2 24.3 reduce-scatter.6
  101.8 73.5 reduce-scatter.8
  178.1 18.6 reduce-scatter.10
